TPU v7x, 32 devices: a whole 2x2x4 slice. The times are simulated.
32 devices in a mesh: row: 8 (over y, x, core), col: 4 (over z).
Axes of the slice: x: 2, y: 2, z: 4, core: 2. Of those that a mesh axis runs over, the one named last changes fastest.
Arguments:
- gate_feats: bfloat16 [8, 4, 1024, 256], P('row', 'col'), may hold values from -6 to 6
- adjacency: int32 [8, 4, 8, 5, 128, 128], P('row', 'col'), may hold values 0 or 1
- gate_count: int32 [8, 4], P('row', 'col'), may hold values from 128 to 1024, as said below
- membership: int32 [8, 4, 512, 1024], P('row', 'col'), may hold values 0 or 1
- tok_count: int32 [8, 4], P('row', 'col'), may hold values from 64 to 512, as said below
- w_msg: bfloat16 [256, 256], replicated, may hold values from -0.375 to 0.375
- w_query: bfloat16 [256, 256], replicated, may hold values from -0.375 to 0.375
- w_key: bfloat16 [256, 256], replicated, may hold values from -0.375 to 0.375
- w_value: bfloat16 [256, 256], replicated, may hold values from -0.375 to 0.375
- w_out: bfloat16 [256, 256], replicated, may hold values from -0.375 to 0.375
- w_score: bfloat16 [256], replicated, may hold values from -0.375 to 0.375
- cotangent: float32 [8, 4, 512], P('row', 'col'), may hold values from -6 to 6
Outputs:
- value_out: float32 [8, 4, 512], P('row', 'col')
- g_msg: float32 [256, 256], replicated
- g_query: float32 [256, 256], replicated
- g_key: float32 [256, 256], replicated
- g_value: float32 [256, 256], replicated
- g_out: float32 [256, 256], replicated
- g_score: float32 [256], replicated
Inputs may be any that keep to these rules, and one draw needn't show every extreme that they name: `gate_count`: some tile is full in every draw. `tok_count`: some tile is full in every draw.
All inputs are finite; a program needn't handle non-finite values. No bound on the sum of `adjacency` or of `membership` on one device may be relied on, other than what follows from the above.
Results may differ from a plain program's by a relative error of at most 0.017.
Values may be sent and summed in bfloat16 or wider, within the bound.
A program may use at most 128 MiB of HBM per device.

v0:
```python
import math

import jax
import jax.numpy as jnp
from jax import lax
from jax.sharding import PartitionSpec as P

H = 256
HEADS = 2
HD = 128
BLK = 128
NB = 8
NT = 512


EPS = 1e-06


def with_halo(array, sides, width):
    for axis, dim in sides:
        size, length = (lax.axis_size(axis), array.shape[dim])
        up = [(i, (i + 1) % size) for i in range(size - 1)]
        down = [(j, i) for i, j in up]
        last = lax.slice_in_dim(array, length - width, length, axis=dim)
        first = lax.slice_in_dim(array, 0, width, axis=dim)
        before = lax.ppermute(last, axis, up)
        after = lax.ppermute(first, axis, down)
        array = jnp.concatenate([before, array, after], axis=dim)
    return array


def silu_grad(preact):
    sigmoid_val = jax.nn.sigmoid(preact)
    return sigmoid_val * (1.0 + preact * (1.0 - sigmoid_val))


def rms_forward(values_in):
    rscale = lax.rsqrt(jnp.mean(values_in * values_in, axis=-1, keepdims=True) + EPS)
    return (values_in * rscale, rscale)


def rms_backward(grad_in, normed, rscale):
    return rscale * (grad_in - normed * jnp.mean(grad_in * normed, axis=-1, keepdims=True))


def split_heads(rows_in):
    return rows_in.reshape(rows_in.shape[0], HEADS, HD)


def score_probs(query_rows, key_rows):
    scores = jnp.einsum(
        "qhd,khd->hqk",
        split_heads(query_rows),
        split_heads(key_rows),
        preferred_element_type=jnp.float32,
    )
    return jax.nn.sigmoid(scores / math.sqrt(HD) - math.log(NT))


def attend_sum(query_rows, key_rows, value_rows):
    weights = score_probs(query_rows, key_rows).astype(jnp.bfloat16)
    output = jnp.einsum(
        "hqk,khd->qhd", weights, split_heads(value_rows), preferred_element_type=jnp.float32
    )
    return output.reshape(query_rows.shape[0], H)


def score_grads(query_rows, grad_rows, key_rows, value_rows):
    probs_val = score_probs(query_rows, key_rows)
    grad_prob = jnp.einsum(
        "qhd,khd->hqk",
        split_heads(grad_rows),
        split_heads(value_rows),
        preferred_element_type=jnp.float32,
    )
    grad_score = (grad_prob * probs_val * (1.0 - probs_val) / math.sqrt(HD)).astype(jnp.bfloat16)
    return (probs_val.astype(jnp.bfloat16), grad_score)


def query_grad(query_rows, grad_rows, key_rows, value_rows):
    weights, grad_score = score_grads(query_rows, grad_rows, key_rows, value_rows)
    grad_query = jnp.einsum(
        "hqk,khd->qhd", grad_score, split_heads(key_rows), preferred_element_type=jnp.float32
    )
    return grad_query.reshape(query_rows.shape[0], H)


def key_value_grads(query_rows, grad_rows, key_rows, value_rows):
    weights, grad_score = score_grads(query_rows, grad_rows, key_rows, value_rows)
    grad_key = jnp.einsum(
        "hqk,qhd->khd", grad_score, split_heads(query_rows), preferred_element_type=jnp.float32
    )
    grad_val = jnp.einsum(
        "hqk,qhd->khd", weights, split_heads(grad_rows), preferred_element_type=jnp.float32
    )
    return jnp.concatenate(
        [grad_key.reshape(key_rows.shape[0], H), grad_val.reshape(key_rows.shape[0], H)], axis=1
    )


def project(rows_in, weight_mat):
    return jnp.dot(rows_in, weight_mat, preferred_element_type=jnp.float32).astype(jnp.bfloat16)


def body(
    gate_feats,
    adjacency,
    gate_count,
    membership,
    tok_count,
    w_msg,
    w_query,
    w_key,
    w_value,
    w_out,
    w_score,
    cotangent,
):
    gate_total = gate_feats.shape[2]
    gate_live = (jnp.arange(gate_total) < gate_count[0, 0]).astype(jnp.float32)
    live_feats = (gate_feats[0, 0].astype(jnp.float32) * gate_live[:, None]).astype(jnp.bfloat16)
    padded = with_halo(live_feats[None, None], (("row", 0), ("col", 1)), 1)
    sources = jnp.stack(
        [padded[1, 1], padded[0, 1], padded[2, 1], padded[1, 0], padded[1, 2]], axis=0
    )
    sources = sources.reshape(5, NB, BLK, H)
    adj_tiles = adjacency[0, 0]
    aggregate = jnp.einsum(
        "bkij,kbjh->bih",
        adj_tiles.astype(jnp.bfloat16),
        sources,
        preferred_element_type=jnp.float32,
    )
    degree = jnp.sum(adj_tiles, axis=(1, 3)).astype(jnp.float32)
    message = (aggregate / (degree[:, :, None] + 1.0)).astype(jnp.bfloat16).reshape(gate_total, H)
    preact = jnp.dot(message, w_msg, preferred_element_type=jnp.float32)
    hidden = (gate_live[:, None] * (live_feats.astype(jnp.float32) + jax.nn.silu(preact))).astype(
        jnp.bfloat16
    )
    member_rows = membership[0, 0].astype(jnp.bfloat16)
    member_count = jnp.sum(membership[0, 0], axis=1).astype(jnp.float32)[:, None]
    pooled = jnp.dot(member_rows, hidden, preferred_element_type=jnp.float32) / (member_count + 1.0)
    normed, rscale = rms_forward(pooled)
    token_live = (jnp.arange(NT) < tok_count[0, 0]).astype(jnp.float32)[:, None]
    tokens = (token_live * normed).astype(jnp.bfloat16)
    query_own = project(tokens, w_query)
    zero_rows = jnp.zeros((NT, H), jnp.float32)
    key_own = project(tokens, w_key)
    value_own = project(tokens, w_value)
    attended = attend_sum(
        query_own,
        lax.all_gather(key_own, "col", axis=0, tiled=True),
        lax.all_gather(value_own, "col", axis=0, tiled=True),
    )
    attended = attended.astype(jnp.bfloat16)
    proj = jnp.dot(attended, w_out, preferred_element_type=jnp.float32)
    pnormed, pscale = rms_forward(proj)
    mixed = tokens.astype(jnp.float32) + pnormed
    score_w = w_score.astype(jnp.float32)
    value_out = token_live[:, 0] * jnp.sum(mixed * score_w, axis=1)
    loss_weight = 1.0 / math.sqrt(lax.axis_size("row") * lax.axis_size("col") * NT)
    grad_value = token_live[:, 0] * cotangent[0, 0] * loss_weight
    g_score = jnp.sum(mixed * grad_value[:, None], axis=0)
    grad_mixed = grad_value[:, None] * score_w
    grad_proj = rms_backward(grad_mixed, pnormed, pscale).astype(jnp.bfloat16)
    g_out = jnp.einsum("nh,ne->he", attended, grad_proj, preferred_element_type=jnp.float32)
    grad_attn = jnp.dot(grad_proj, w_out.T, preferred_element_type=jnp.float32).astype(jnp.bfloat16)
    key_all, value_all = (
        lax.all_gather(key_own, "col", axis=0, tiled=True),
        lax.all_gather(value_own, "col", axis=0, tiled=True),
    )

    def add_query(running, pair_in):
        return (running + query_grad(query_own, grad_attn, pair_in[0], pair_in[1]), 0)

    grad_query, unused = lax.scan(
        add_query, zero_rows, (key_all.reshape(-1, NT, H), value_all.reshape(-1, NT, H))
    )
    key_part = key_all.reshape(lax.axis_size("col") * NT // NT, NT, H)
    value_part = value_all.reshape(lax.axis_size("col") * NT // NT, NT, H)
    terms = lax.map(
        lambda pair_in: key_value_grads(query_own, grad_attn, pair_in[0], pair_in[1]),
        (key_part, value_part),
    )
    key_sums = lax.psum_scatter(
        terms.reshape(lax.axis_size("col") * NT, 2 * H), "col", scatter_dimension=0, tiled=True
    )
    grad_query = grad_query.astype(jnp.bfloat16)
    grad_key = key_sums[:, :H].astype(jnp.bfloat16)
    grad_val = key_sums[:, H:].astype(jnp.bfloat16)
    g_query = jnp.einsum("nh,ne->he", tokens, grad_query, preferred_element_type=jnp.float32)
    g_key = jnp.einsum("nh,ne->he", tokens, grad_key, preferred_element_type=jnp.float32)
    g_value = jnp.einsum("nh,ne->he", tokens, grad_val, preferred_element_type=jnp.float32)
    grad_tokens = grad_mixed + jnp.dot(grad_query, w_query.T, preferred_element_type=jnp.float32)
    grad_tokens = grad_tokens + jnp.dot(grad_key, w_key.T, preferred_element_type=jnp.float32)
    grad_tokens = grad_tokens + jnp.dot(grad_val, w_value.T, preferred_element_type=jnp.float32)
    grad_pooled = rms_backward(token_live * grad_tokens, normed, rscale)
    grad_scaled = (grad_pooled / (member_count + 1.0)).astype(jnp.bfloat16)
    grad_hidden = jnp.einsum(
        "ng,nh->gh", member_rows, grad_scaled, preferred_element_type=jnp.float32
    )
    grad_pre = (gate_live[:, None] * grad_hidden * silu_grad(preact)).astype(jnp.bfloat16)
    g_msg = jnp.einsum("gh,ge->he", message, grad_pre, preferred_element_type=jnp.float32)
    summed = lax.psum((g_msg, g_query, g_key, g_value, g_out, g_score), ("row", "col"))
    return (value_out[None, None], summed[0], summed[1], summed[2], summed[3], summed[4], summed[5])


def solution(mesh):
    placed = (
        P("row", "col", None, None),
        P("row", "col", None, None, None, None),
        P("row", "col"),
        P("row", "col", None, None),
        P("row", "col"),
        P(),
        P(),
        P(),
        P(),
        P(),
        P(),
        P("row", "col", None),
    )
    return jax.shard_map(
        body,
        mesh=mesh,
        in_specs=placed,
        out_specs=(P("row", "col", None), P(), P(), P(), P(), P(), P()),
        check_vma=False,
    )
```

profile of v0, /device:TPU:0, one launch (start us, length us, event | category | flops | bytes accessed | tf_op | source)
XLA Modules:
  0.0 403.7 jit_solution(3272286056454183889)
XLA Ops:
  7.9 1.4 multiply_convert_fusion.3
  9.3 2.4 collective-permute-start
  11.7 1.3 collective-permute-start.1
  13.2 4.4 %collective-permute-done.1 = bf16[1,1,1024,256]{3,2,1,0:T(8,128)(2,1)S(1)} collective-permute-done((bf16[1,1,1024,256]{3,2,1,0:T(8,128)(2,1)S(1)}, bf16[1,1,1024,256]{3,2,1,0:T(8,128)(2,1)S(1)}, u32[]{:S(2)}, u32[]{:S(2)}) %collective-permute-start.1) | collective-permute-done | bytes 524320 | tf_op jit(solution)/shard_map/ppermute | solution.py:27
  17.6 1.4 pad_maximum_fusion
  19.0 4.8 %collective-permute-start.2 = (bf16[3,1,1024,256]{3,2,1,0:T(8,128)(2,1)}, bf16[3,1,1024,256]{3,2,1,0:T(8,128)(2,1)}, u32[]{:S(2)}, u32[]{:S(2)}) collective-permute-start(bf16[3,1,1024,256]{3,2,1,0:T(8,128)(2,1)} %pad_maximum_fusion), channel_id=1, source_target_pairs={{0,1},{1,2},{2,3},{4,5},{5,6},{6,7},{8,9},{9,10},{10,11},{12,13},{... | collective-permute-start | bytes 4718600 | tf_op jit(solution)/shard_map/ppermute | solution.py:26
  23.8 1.3 collective-permute-start.3
  25.3 1.8 reduce_sum.75
  28.0 1.1 constant_dynamic-update-slice_fusion.4
  29.2 18.9 %collective-permute-done.2 = bf16[3,1,1024,256]{3,2,1,0:T(8,128)(2,1)} collective-permute-done((bf16[3,1,1024,256]{3,2,1,0:T(8,128)(2,1)}, bf16[3,1,1024,256]{3,2,1,0:T(8,128)(2,1)}, u32[]{:S(2)}, u32[]{:S(2)}) %collective-permute-start.2) | collective-permute-done | bytes 1572896 | tf_op jit(solution)/shard_map/ppermute | solution.py:26
  48.1 1.1 slice.18
  49.2 4.7 %collective-permute-done.3 = bf16[3,1,1024,256]{3,2,1,0:T(8,128)(2,1)} collective-permute-done((bf16[3,1,1024,256]{3,2,1,0:T(8,128)(2,1)}, bf16[3,1,1024,256]{3,2,1,0:T(8,128)(2,1)}, u32[]{:S(2)}, u32[]{:S(2)}) %collective-permute-start.3) | collective-permute-done | bytes 1572896 | tf_op jit(solution)/shard_map/ppermute | solution.py:27
  54.0 1.1 slice.19
  57.9 1.0 convolution_convert_fusion.3
  58.9 1.0 convolution_convert_fusion.1
  60.3 41.9 %all-gather.3.cloned.1.call-done = bf16[2048,256]{1,0:T(8,128)(2,1)} async-done(((bf16[512,256]{1,0:T(8,128)(2,1)}), bf16[2048,256]{1,0:T(8,128)(2,1)}) %all-gather.3.cloned.1.call-update) | async-done | bytes 1048592 | tf_op jit(solution)/shard_map/all_gather | solution.py:153
  102.2 1.5 copy.43
  103.7 28.1 %all-gather.5.cloned.1.call-done = bf16[2048,256]{1,0:T(8,128)(2,1)} async-done(((bf16[512,256]{1,0:T(8,128)(2,1)}), bf16[2048,256]{1,0:T(8,128)(2,1)}) %all-gather.5.cloned.1.call-update) | async-done | bytes 1048592 | tf_op jit(solution)/shard_map/all_gather | solution.py:152
  131.8 2.3 copy.44
  134.1 4.8 %fusion.32 = bf16[2,128,512]{2,1,0:T(8,128)(2,1)S(1)} fusion(bf16[2048,2,128]{0,2,1:T(8,128)(2,1)S(1)} %bitcast.196, bf16[512,2,128]{0,2,1:T(8,128)(2,1)S(1)} %bitcast.182, bf16[2048,2,128]{0,2,1:T(8,128)(2,1)} %bitcast.197), kind=kOutput, calls=%fused_computation.45 | convolution fusion | flops 1086455808 | bytes 2621440 | tf_op jit(solution)/shard_map/hqk,khd->qhd/dot_general | solution.py:62
  140.1 1.1 convolution_convert_fusion
  141.2 1.1 copy.32
  142.3 1.3 copy.30
  143.6 26.3 %while.25 = (s32[]{:T(128)}, f32[4,512,512]{2,1,0:T(8,128)}, bf16[4,512,256]{2,1,0:T(8,128)(2,1)}, bf16[512,256]{0,1:T(8,128)(2,1)S(1)}, bf16[4,512,256]{1,2,0:T...) while((s32[]{:T(128)}, f32[4,512,512]{2,1,0:T(8,128)}, bf16[4,512,256]{2,1,0:T(8,128)(2,1)}, ...), condition=%wide.region_9.10_spmd, body=%wide.region_8.9_spmd.sunk | while | flops 542900224 | bytes 18875020 | solution.py:181
  143.7 1.1 constant_dynamic-slice_fusion.8
  145.5 1.0 constant_dynamic-slice_fusion.9
  146.6 1.7 fusion.152
  149.2 1.1 constant_dynamic-update-slice_fusion.6
  150.3 1.1 constant_dynamic-slice_fusion.8
  152.1 1.0 constant_dynamic-slice_fusion.9
  153.2 1.7 fusion.152
  155.8 1.0 constant_dynamic-update-slice_fusion.6
  156.8 1.1 constant_dynamic-slice_fusion.8
  159.7 1.7 fusion.152
  162.3 1.1 constant_dynamic-update-slice_fusion.6
  163.4 1.1 constant_dynamic-slice_fusion.8
  166.3 1.7 fusion.152
  168.9 1.0 constant_dynamic-update-slice_fusion.6
  171.1 27.1 %while.26 = (s32[]{:T(128)}, f32[512,256]{0,1:T(8,128)S(1)}, bf16[4,512,256]{1,2,0:T(8,128)(2,1)}, bf16[4,512,256]{2,1,0:T(8,128)(2,1)}, bf16[512,256]{1,0:T(8,1...) while((s32[]{:T(128)}, f32[512,256]{0,1:T(8,128)S(1)}, ...), condition=%wide.region_7.8_spmd.clone, body=%wide.region_6.7_spmd.clone.sunk | while | flops 408158208 | bytes 9437287 | solution.py:176
  172.1 1.1 copy.74
  173.6 1.7 constant_dynamic-slice_fusion.10
  175.3 2.5 fusion.160
  179.0 1.1 copy.74
  180.5 1.7 constant_dynamic-slice_fusion.10
  182.2 2.3 fusion.160
  184.7 1.0 constant_dynamic-slice_fusion.11
  185.8 1.1 copy.74
  187.3 1.7 constant_dynamic-slice_fusion.10
  188.9 2.3 fusion.160
  192.5 1.1 copy.74
  194.0 1.7 constant_dynamic-slice_fusion.10
  195.7 2.3 fusion.160
  199.1 2.1 fusion.91
  201.3 45.1 %reduce-scatter.2.cloned.1.call-done = f32[512,512]{1,0:T(8,128)} async-done(((f32[2048,512]{1,0:T(8,128)}), f32[512,512]{1,0:T(8,128)}) %reduce-scatter.2.cloned.1.call-update) | async-done | bytes 1048592 | tf_op jit(solution)/shard_map/reduce_scatter | solution.py:185
  246.4 1.3 convert.6
  249.6 1.3 fusion.74
  251.2 1.1 fusion.49
  252.4 3.2 fusion.28
  255.7 40.9 %psum.47 = f32[256]{0:T(256)} all-reduce(f32[256]{0:T(256)S(1)} %copy-done.30), channel_id=1, replica_groups=mesh['row'=8,'col'=4] {'row','col'}, use_global_device_ids=true, to_apply=%region_18.19 | all-reduce | flops 256 | bytes 2048 | tf_op jit(solution)/shard_map/psum | solution.py:204
  297.2 92.5 %all-reduce.3.cloned.1.call-done = (f32[256,256]{1,0:T(8,128)}, f32[256,256]{1,0:T(8,128)}, f32[256,256]{1,0:T(8,128)}, f32[256,256]{1,0:T(8,128)}, f32[256,256]{1,0:T(8,128)}) async-done(((f32[256,256]{1,0:T(8,128)}, f32[256,256]{1,0:T(8,128)}, f32[256,256]{1,0:T(8,128)}, f32[256,256]{1,0:T(8,128)}, f32[256,256]{1,0:T(8,128)}), (f32[256,256]{1,0:T(8,128)}, f32[256,256]{1,0:T(8,128)}, f32[256,256]{1,0:T(8,128)}, ...) | async-done | bytes 1310736 | tf_op jit(solution)/shard_map/psum | solution.py:204
  389.7 1.7 copy.99
  391.4 1.7 copy.100
  393.1 1.7 copy.101
  394.7 1.7 copy.102
  (160 shorter events, 24.9 us)
Async XLA Ops:
  7.2 131.8 %copy-start = (bf16[256,256]{1,0:T(8,128)(2,1)S(1)}, bf16[256,256]{1,0:T(8,128)(2,1)}, u32[]{:S(2)}) copy-start(bf16[256,256]{1,0:T(8,128)(2,1)} %param.25) | copy-start | bytes 393220
  7.2 95.0 %all-gather.3.cloned.1.call-start = ((), (), s32[]{:S(2)}) async-start(), calls=%async_computation.1 | async-start | bytes 1310720 | tf_op jit(solution)/shard_map/all_gather | solution.py:153
  7.9 48.4 %copy-start.24 = (f32[1024]{0:T(1024)}, f32[1024]{0:T(1024)S(1)}, u32[]{:S(2)}) copy-start(f32[1024]{0:T(1024)S(1)} %fusion.84) | copy-start | bytes 12292
  7.9 17.1 %copy-start.7 = (s32[1,1,8,5,128,128]{5,4,3,2,1,0:T(8,128)S(1)}, s32[1,1,8,5,128,128]{5,4,3,2,1,0:T(8,128)}, u32[]{:S(2)}) copy-start(s32[1,1,8,5,128,128]{5,4,3,2,1,0:T(8,128)} %param.17) | copy-start | bytes 7864324
  9.3 3.9 collective-permute-start
  11.7 5.9 %collective-permute-start.1 = (bf16[1,1,1024,256]{3,2,1,0:T(8,128)(2,1)S(1)}, bf16[1,1,1024,256]{3,2,1,0:T(8,128)(2,1)S(1)}, u32[]{:S(2)}, u32[]{:S(2)}) collective-permute-start(bf16[1,1,1024,256]{3,2,1,0:T(8,128)(2,1)S(1)} %multiply_convert_fusion.3), channel_id=1, source_target_pairs={{4,0},{8,4},{12,8},{16,12},{20,16},{24,20},{28,24},{5,1},{9,5},{13... | collective-permute-start | bytes 1572872 | tf_op jit(solution)/shard_map/ppermute | solution.py:27
  13.2 4.4 %copy-start.11 = (bf16[1,1,1024,256]{3,2,1,0:T(8,128)(2,1)}, bf16[1,1,1024,256]{3,2,1,0:T(8,128)(2,1)S(1)}, u32[]{:S(2)}) copy-start(bf16[1,1,1024,256]{3,2,1,0:T(8,128)(2,1)S(1)} %collective-permute-done) | copy-start | bytes 1572868
  17.6 1.4 copy-start.12
  19.0 8.8 %copy-start.10 = (bf16[1,1,1024,256]{3,2,1,0:T(8,128)(2,1)S(1)}, bf16[1,1,1024,256]{3,2,1,0:T(8,128)(2,1)}, u32[]{:S(2)}) copy-start(bf16[1,1,1024,256]{3,2,1,0:T(8,128)(2,1)} %param.16) | copy-start | bytes 1572868
  19.0 29.1 %collective-permute-start.2 = (bf16[3,1,1024,256]{3,2,1,0:T(8,128)(2,1)}, bf16[3,1,1024,256]{3,2,1,0:T(8,128)(2,1)}, u32[]{:S(2)}, u32[]{:S(2)}) collective-permute-start(bf16[3,1,1024,256]{3,2,1,0:T(8,128)(2,1)} %pad_maximum_fusion), channel_id=1, source_target_pairs={{0,1},{1,2},{2,3},{4,5},{5,6},{6,7},{8,9},{9,10},{10,11},{12,13},{... | collective-permute-start | bytes 4718600 | tf_op jit(solution)/shard_map/ppermute | solution.py:26
  23.8 30.2 %collective-permute-start.3 = (bf16[3,1,1024,256]{3,2,1,0:T(8,128)(2,1)}, bf16[3,1,1024,256]{3,2,1,0:T(8,128)(2,1)}, u32[]{:S(2)}, u32[]{:S(2)}) collective-permute-start(bf16[3,1,1024,256]{3,2,1,0:T(8,128)(2,1)} %pad_maximum_fusion), channel_id=1, source_target_pairs={{1,0},{2,1},{3,2},{5,4},{6,5},{7,6},{9,8},{10,9},{11,10},{13,12},{... | collective-permute-start | bytes 4718600 | tf_op jit(solution)/shard_map/ppermute | solution.py:27
  27.1 2.1 copy-start.13
  27.8 28.5 %copy-start.32 = (f32[512]{0:T(512)}, f32[512]{0:T(512)S(1)}, u32[]{:S(2)}) copy-start(f32[512]{0:T(512)S(1)} %convert_add_fusion.2) | copy-start | bytes 6148
  55.1 0.9 copy-start.23
  55.1 1.7 copy-start.8
  55.8 1.8 copy-start.21
  56.8 1.0 copy-start.15
  56.8 1.1 copy-start.16
  56.8 2.2 copy-start.17
  57.8 81.5 %copy-start.3 = (f32[256,512]{1,0:T(8,128)}, f32[256,512]{1,0:T(8,128)S(1)}, u32[]{:S(2)}) copy-start(f32[256,512]{1,0:T(8,128)S(1)} %get-tuple-element.241) | copy-start | bytes 1572868
  57.8 2.2 copy-start.34
  57.8 2.2 copy-start.31
  57.8 2.3 copy-start.19
  58.9 72.9 %all-gather.5.cloned.1.call-start = ((), (), s32[]{:S(2)}) async-start(), calls=%async_computation.2 | async-start | bytes 1310720 | tf_op jit(solution)/shard_map/all_gather | solution.py:152
  59.9 186.5 %reduce-scatter.2.cloned.1.call-start = ((), (), s32[]{:S(2)}) async-start(), calls=%async_computation.3 | async-start | bytes 5242880 | tf_op jit(solution)/shard_map/reduce_scatter | solution.py:185
  60.0 80.1 %copy-start.26 = (f32[256]{0:T(256)}, f32[256]{0:T(256)S(1)}, u32[]{:S(2)}) copy-start(f32[256]{0:T(256)S(1)} %convert_element_type.188) | copy-start | bytes 3076
  138.9 4.7 %copy-start.14 = (bf16[2,128,512]{2,1,0:T(8,128)(2,1)}, bf16[2,128,512]{2,1,0:T(8,128)(2,1)S(1)}, u32[]{:S(2)}) copy-start(bf16[2,128,512]{2,1,0:T(8,128)(2,1)S(1)} %fusion.32) | copy-start | bytes 786436
  138.9 3.4 copy-start.6
  139.2 4.4 %copy-start.5 = (f32[512,256]{0,1:T(8,128)}, f32[512,256]{0,1:T(8,128)S(1)}, u32[]{:S(2)}) copy-start(f32[512,256]{0,1:T(8,128)S(1)} %get-tuple-element.243) | copy-start | bytes 1572868
  140.1 3.5 copy-start.29
  143.7 1.9 copy-start.1
  148.8 1.4 copy-start.2
  150.3 1.8 copy-start.1
  155.4 1.4 copy-start.2
  156.8 1.8 copy-start.1
  162.0 1.4 copy-start.2
  163.4 1.8 copy-start.1
  168.6 1.4 copy-start.2
  170.0 219.7 %all-reduce.3.cloned.1.call-start = ((), (), s32[]{:S(2)}) async-start(), calls=%async_computation.4 | async-start | bytes 2621440 | tf_op jit(solution)/shard_map/psum | solution.py:204
  201.3 49.9 %copy-start.4 = (f32[256,512]{1,0:T(8,128)S(1)}, f32[256,512]{1,0:T(8,128)}, u32[]{:S(2)}) copy-start(f32[256,512]{1,0:T(8,128)} %copy-done.3) | copy-start | bytes 1572868
  201.3 49.9 %copy-start.27 = (f32[256]{0:T(256)S(1)}, f32[256]{0:T(256)}, u32[]{:S(2)}) copy-start(f32[256]{0:T(256)} %copy-done.26) | copy-start | bytes 3076
  246.4 4.5 %copy-start.18 = (bf16[256,256]{1,0:T(8,128)(2,1)S(1)}, bf16[256,256]{1,0:T(8,128)(2,1)}, u32[]{:S(2)}) copy-start(bf16[256,256]{1,0:T(8,128)(2,1)} %param.23) | copy-start | bytes 393220
  246.4 4.8 %copy-start.20 = (bf16[256,256]{1,0:T(8,128)(2,1)S(1)}, bf16[256,256]{1,0:T(8,128)(2,1)}, u32[]{:S(2)}) copy-start(bf16[256,256]{1,0:T(8,128)(2,1)} %param.22) | copy-start | bytes 393220
  249.6 2.7 copy-start.9
  249.6 2.7 copy-start.25
  249.6 2.7 copy-start.33
  252.4 3.3 copy-start.30
  252.4 44.2 %copy-start.28 = (f32[512]{0:T(512)S(1)}, f32[512]{0:T(512)}, u32[]{:S(2)}) copy-start(f32[512]{0:T(512)} %get-tuple-element.209) | copy-start | bytes 6148
  389.7 6.7 %copy-start.22 = (f32[256,256]{1,0:T(8,128)S(1)}, f32[256,256]{1,0:T(8,128)}, u32[]{:S(2)}) copy-start(f32[256,256]{1,0:T(8,128)} %get-tuple-element.370) | copy-start | bytes 786436
Sparse Core Ops, SparseCore 0:
  59.0 43.1 all-gather.2
  104.3 27.4 all-gather.4
  170.1 76.2 reduce-scatter.1
  255.8 133.8 all-reduce.2
where the time goes:
time: 405 us; the launch traced here: 404 us
  waiting for transfers between devices  236 us (58%)
  local copies, waits for them, and re-layouts  48 us (12%)
  matrix products  43.8 us (11%)
  blocking collectives  40.9 us (10%)
  between operations  15.7 us (4%)
  starting transfers between devices  10.1 us (2%)
  other arithmetic  8.72 us (2%)
    psum x1, waiting for transfers between devices, body(): lax.psum((g_msg, g_query, g_key, g_value, g_out, g_score), ('row', 'col'))  92.5 us
    reduce_scatter x1, waiting for transfers between devices, body(): lax.psum_scatter(terms.reshape(lax.axis_size('col') * NT, 2 * H), 'col',...  45.1 us
    all_gather x1, waiting for transfers between devices, body(): lax.all_gather(value_own, 'col', axis=0, tiled=True)  41.9 us
    psum x1, blocking collectives, body(): lax.psum((g_msg, g_query, g_key, g_value, g_out, g_score), ('row', 'col'))  40.9 us
    all_gather x1, waiting for transfers between devices, body(): lax.all_gather(key_own, 'col', axis=0, tiled=True)  28.1 us
    ppermute x2, waiting for transfers between devices, with_halo(): before = lax.ppermute(last, axis, up)  19.1 us
    dynamic_slice x16, local copies, waits for them, and re-layouts, body(): lax.scan(add_query, zero_rows, (key_all.reshape(-1, NT, H), value_all.res...  18.7 us
    unnamed x76, local copies, waits for them, and re-layouts  11.7 us
  transfers between devices with their start and end apart: 8, of which 8 were waited for; matrix products, arithmetic and copies ran while one was open for 10% of the time, Pallas kernels for 0%

commit v1 on v0

v1 whole, which is shorter than its diff:
```python
import math

import jax
import jax.numpy as jnp
from jax import lax
from jax.experimental import pallas as pl
from jax.experimental.pallas import tpu as pltpu
from jax.sharding import PartitionSpec as P

H = 256
HEADS = 2
HD = 128
BLK = 128
NB = 8
NT = 512
G = NB * BLK
NCH = 4
CG = G // NCH
EPS = 1e-06
F32 = jnp.float32
BF16 = jnp.bfloat16
MESH = pl.DeviceIdType.MESH


def mm(a, b):
    return jnp.dot(a, b, preferred_element_type=F32)


def mm_nt(a, b):
    return lax.dot_general(a, b, (((1,), (1,)), ((), ())), preferred_element_type=F32)


def mm_tn(a, b):
    return lax.dot_general(a, b, (((0,), (0,)), ((), ())), preferred_element_type=F32)


def remote(src, dst, send, recv, axis, peer):
    return pltpu.make_async_remote_copy(
        src_ref=src, dst_ref=dst, send_sem=send, recv_sem=recv,
        device_id={axis: peer}, device_id_type=MESH,
    )


def others(size, func):
    def step(s, carry):
        func(s)
        return carry

    lax.fori_loop(1, size, step, 0)


def rms_forward(values_in):
    rscale = lax.rsqrt(jnp.mean(values_in * values_in, axis=-1, keepdims=True) + EPS)
    return (values_in * rscale, rscale)


def rms_backward(grad_in, normed, rscale):
    return rscale * (grad_in - normed * jnp.mean(grad_in * normed, axis=-1, keepdims=True))


def prob_parts(scores):
    expo = math.log2(NT) - scores * (math.log2(math.e) / math.sqrt(HD))
    power = jnp.exp2(jnp.minimum(expo, 120.0))
    prob = pl.reciprocal(1.0 + power, approx=True)
    return prob, prob * (prob * power) * (1.0 / math.sqrt(HD))


def kernel(
    rows, cols,
    gate_count, tok_count, feats_hbm, adj_hbm, mem_hbm,
    w_msg, w_query, w_key, w_value, w_out, w_score, cot,
    value_out, g_msg, g_query, g_key, g_value, g_out, g_score,
    feats, live, halo, adj_i, mem_i, adj, inv_deg, mem, mem_t, inv_cnt,
    message, preact, pooled, normed, rscale,
    tok, q_all, k_all, v_all, ga_all, d_own, p_t, d_t, att, gq, gk, gv, gmix,
    sa, ra, sb, rb, sc, rc, ta, ua, tb, ub, tc, uc, fa, fb, fc,
    local_sem, halo_s, halo_r, tok_s, tok_r, ga_s, ga_r,
    one_s, one_r, two_s, two_r, three_s, three_r,
):
    r = lax.axis_index("row")
    c = lax.axis_index("col")
    ch = H // rows

    load_feats = pltpu.make_async_copy(feats_hbm, feats, local_sem.at[0])
    load_adj = pltpu.make_async_copy(adj_hbm, adj_i, local_sem.at[1])
    load_mem = pltpu.make_async_copy(mem_hbm, mem_i, local_sem.at[2])
    load_feats.start()
    load_adj.start()
    load_mem.start()

    barrier = pltpu.get_barrier_semaphore()
    others(rows, lambda s: pl.semaphore_signal(
        barrier, inc=1, device_id={"row": lax.rem(r + s, rows)}, device_id_type=MESH))
    others(cols, lambda s: pl.semaphore_signal(
        barrier, inc=1, device_id={"col": lax.rem(c + s, cols)}, device_id_type=MESH))

    gates = gate_count[0, 0]
    load_feats.wait()
    for i in range(NCH):
        alive = (lax.broadcasted_iota(jnp.int32, (CG, 1), 0) + i * CG < gates).astype(F32)
        live[i] = (feats[i * CG:(i + 1) * CG].astype(F32) * alive).astype(BF16)
    pl.semaphore_wait(barrier, rows + cols - 2)

    ways = (
        (2, "col", 1, c < cols - 1, c > 0),
        (3, "col", -1, c > 0, c < cols - 1),
        (0, "row", 1, r < rows - 1, r > 0),
        (1, "row", -1, r > 0, r < rows - 1),
    )
    place = {"row": r, "col": c}

    def halo_copy(way, i):
        slot, axis, step, _, _ = way
        return remote(live.at[i], halo.at[slot, i], halo_s.at[slot, i], halo_r.at[slot, i],
                      axis, place[axis] + step)

    for way in ways:
        @pl.when(jnp.logical_not(way[4]))
        def _(way=way):
            halo[way[0]] = jnp.zeros((NCH, CG, H), BF16)

        @pl.when(way[3])
        def _(way=way):
            for i in range(NCH):
                halo_copy(way, i).start()

    load_adj.wait()

    def adj_step(b, carry):
        parts = [adj_i[b, k].astype(F32) for k in range(5)]
        total = parts[0] + parts[1] + parts[2] + parts[3] + parts[4]
        inv_deg[b] = 1.0 / (jnp.sum(total, axis=1, keepdims=True) + 1.0)
        for k in range(5):
            adj[b, :, k * BLK:(k + 1) * BLK] = parts[k].astype(BF16)
        return carry

    lax.fori_loop(0, NB, adj_step, 0)
    load_mem.wait()
    count = jnp.zeros((NT, 1), F32)
    for i in range(NCH):
        part = mem_i[:, i * CG:(i + 1) * CG].astype(F32)
        count = count + jnp.sum(part, axis=1, keepdims=True)
        mem[i] = part.astype(BF16)
        mem_t[i] = part.T.astype(BF16)
    inv_cnt[...] = 1.0 / (count + 1.0)

    pooled[...] = jnp.zeros((NT, H), F32)

    def gate_step(i, carry):
        for way in ways:
            @pl.when(way[4])
            def _(way=way):
                slot, axis, step, _, _ = way
                remote(live.at[i], halo.at[slot, i], halo_s.at[slot, i], halo_r.at[slot, i],
                       axis, place[axis] - step).wait_recv()
        own = live[i]
        for b in range(CG // BLK):
            cut = slice(b * BLK, (b + 1) * BLK)
            blk = i * (CG // BLK) + b
            srcs = jnp.concatenate([own[cut]] + [halo[k, i, cut] for k in range(4)], axis=0)
            message[i, cut] = (mm(adj[blk], srcs) * inv_deg[blk]).astype(BF16)
        pre = mm(message[i], w_msg[...])
        preact[i] = pre
        alive = (lax.broadcasted_iota(jnp.int32, (CG, 1), 0) + i * CG < gates).astype(F32)
        hidden = (alive * (own.astype(F32) + pre / (1.0 + jnp.exp(-pre)))).astype(BF16)
        pooled[...] += mm(mem[i], hidden)
        return carry

    lax.fori_loop(0, NCH, gate_step, 0)

    n_live = tok_count[0, 0]
    tlive = (lax.broadcasted_iota(jnp.int32, (NT, 1), 0) < n_live).astype(F32)
    norm_val, rs_val = rms_forward(pooled[...] * inv_cnt[...])
    normed[...] = norm_val
    rscale[...] = rs_val
    tok[c] = (tlive * norm_val).astype(BF16)

    def tok_copy(peer, slot):
        return remote(tok.at[slot], tok.at[slot], tok_s.at[peer], tok_r.at[slot], "col", peer)

    others(cols, lambda s: tok_copy(lax.rem(c + s, cols), c).start())
    own_tok = tok[c]
    q_all[c] = mm(own_tok, w_query[...]).astype(BF16)
    att[...] = jnp.zeros((NT, H), F32)

    def attend_step(s, carry):
        src = lax.rem(c + s, cols)

        @pl.when(s > 0)
        def _():
            tok_copy(src, src).wait_recv()

        k_all[src] = mm(tok[src], w_key[...]).astype(BF16)
        v_all[src] = mm(tok[src], w_value[...]).astype(BF16)
        for h in range(HEADS):
            lanes = slice(h * HD, (h + 1) * HD)
            prob, slope = prob_parts(mm_nt(q_all[c, :, lanes], k_all[src, :, lanes]))
            d_own[src, h] = slope.astype(BF16)
            att[:, lanes] += mm(prob.astype(BF16), v_all[src, :, lanes])
        return carry

    lax.fori_loop(0, cols, attend_step, 0)

    attended = att[...].astype(BF16)
    pnormed, pscale = rms_forward(mm(attended, w_out[...]))
    mixed = own_tok.astype(F32) + pnormed
    score_w = w_score[...].astype(F32)
    val = tlive * jnp.sum(mixed * score_w, axis=1, keepdims=True)
    value_out[...] = jnp.broadcast_to(val, (NT, 128)).T[0:1]
    cot_col = jnp.broadcast_to(cot[...], (128, NT)).T[:, 0:1]
    grad_value = tlive * cot_col * (1.0 / math.sqrt(rows * cols * NT))
    grad_mixed = grad_value * score_w
    gmix[...] = grad_mixed
    grad_proj = rms_backward(grad_mixed, pnormed, pscale).astype(BF16)
    ga_all[c] = mm_nt(grad_proj, w_out[...]).astype(BF16)

    def ga_copy(peer, slot):
        return remote(ga_all.at[slot], ga_all.at[slot], ga_s.at[peer], ga_r.at[slot], "col", peer)

    others(cols, lambda s: ga_copy(lax.rem(c + s, cols), c).start())

    def one_copy(g, send, recv, peer, slot):
        return remote(send.at[peer], recv.at[slot], one_s.at[g, peer], one_r.at[g, slot], "row", peer)

    def one_start(g, send, recv):
        recv[r] = send[r]
        others(rows, lambda s: one_copy(g, send, recv, lax.rem(r + s, rows), r).start())

    def two_copy(g, send, recv, peer, slot):
        return remote(send, recv.at[slot], two_s.at[g, peer], two_r.at[g, slot], "col", peer)

    def two_start(g, send, recv, mid, gathered):
        others(rows, lambda s: one_copy(
            g, send, recv, lax.rem(r + s, rows), lax.rem(r + s, rows)).wait_recv())
        total = recv[0].astype(F32)
        for p in range(1, rows):
            total = total + recv[p].astype(F32)
        mid[...] = total.astype(BF16)
        gathered[c] = mid[...]
        others(cols, lambda s: two_copy(g, mid, gathered, lax.rem(c + s, cols), c).start())

    def three_copy(g, full, peer, slot):
        return remote(full.at[slot], full.at[slot], three_s.at[g, peer], three_r.at[g, slot],
                      "row", peer)

    def three_start(g, mid, gathered, full, span):
        others(cols, lambda s: two_copy(
            g, mid, gathered, lax.rem(c + s, cols), lax.rem(c + s, cols)).wait_recv())
        total = gathered[0].astype(F32)
        for p in range(1, cols):
            total = total + gathered[p].astype(F32)
        full[r] = total[:span].astype(BF16)
        others(rows, lambda s: three_copy(g, full, lax.rem(r + s, rows), r).start())
        return total

    def three_wait(g, full):
        others(rows, lambda s: three_copy(
            g, full, lax.rem(r + s, rows), lax.rem(r + s, rows)).wait_recv())

    def finish(g, send, recv, mid, gathered, full):
        def row_send(s):
            p = lax.rem(r + s, rows)
            one_copy(g, send, recv, p, r).wait_send()
            three_copy(g, full, p, r).wait_send()

        others(rows, row_send)
        others(cols, lambda s: two_copy(g, mid, gathered, lax.rem(c + s, cols), c).wait_send())

    score_part = jnp.broadcast_to(jnp.sum(mixed * grad_value, axis=0, keepdims=True), (16, H))
    out_part = mm_tn(attended, grad_proj)
    for p in range(rows):
        sa[p, 0:ch] = out_part[p * ch:(p + 1) * ch].astype(BF16)
        sa[p, ch:ch + 16] = score_part.astype(BF16)
    one_start(0, sa, ra)

    gq[...] = jnp.zeros((NT, H), F32)
    gk[...] = jnp.zeros((NT, H), F32)
    gv[...] = jnp.zeros((NT, H), F32)

    def query_step(s, carry):
        src = lax.rem(c + s, cols)
        q_all[src] = mm(tok[src], w_query[...]).astype(BF16)
        for h in range(HEADS):
            lanes = slice(h * HD, (h + 1) * HD)
            grad_prob = mm_nt(ga_all[c, :, lanes], v_all[src, :, lanes])
            grad_score = (grad_prob * d_own[src, h].astype(F32)).astype(BF16)
            gq[:, lanes] += mm(grad_score, k_all[src, :, lanes])
            prob, slope = prob_parts(mm_nt(k_all[c, :, lanes], q_all[src, :, lanes]))
            p_t[src, h] = prob.astype(BF16)
            d_t[src, h] = slope.astype(BF16)
        return carry

    lax.fori_loop(0, cols, query_step, 0)
    two_start(0, sa, ra, ta, ua)

    def key_step(s, carry):
        src = lax.rem(c + s, cols)

        @pl.when(s > 0)
        def _():
            ga_copy(src, src).wait_recv()

        for h in range(HEADS):
            lanes = slice(h * HD, (h + 1) * HD)
            grad_prob = mm_nt(v_all[c, :, lanes], ga_all[src, :, lanes])
            grad_score = (grad_prob * d_t[src, h].astype(F32)).astype(BF16)
            gk[:, lanes] += mm(grad_score, q_all[src, :, lanes])
            gv[:, lanes] += mm(p_t[src, h], ga_all[src, :, lanes])
        return carry

    lax.fori_loop(0, cols, key_step, 0)

    grad_query = gq[...].astype(BF16)
    grad_key = gk[...].astype(BF16)
    grad_val = gv[...].astype(BF16)
    for j, grad in enumerate((grad_query, grad_key, grad_val)):
        part = mm_tn(own_tok, grad).astype(BF16)
        for p in range(rows):
            sb[p, j * ch:(j + 1) * ch] = part[p * ch:(p + 1) * ch]
    one_start(1, sb, rb)

    grad_tokens = gmix[...] + mm_nt(grad_query, w_query[...])
    grad_tokens = grad_tokens + mm_nt(grad_key, w_key[...])
    grad_tokens = grad_tokens + mm_nt(grad_val, w_value[...])
    grad_pooled = rms_backward(tlive * grad_tokens, normed[...], rscale[...])
    grad_scaled = (grad_pooled * inv_cnt[...]).astype(BF16)
    msg_part = jnp.zeros((H, H), F32)
    for i in range(NCH):
        alive = (lax.broadcasted_iota(jnp.int32, (CG, 1), 0) + i * CG < gates).astype(F32)
        pre = preact[i]
        sig = 1.0 / (1.0 + jnp.exp(-pre))
        grad_pre = alive * mm(mem_t[i], grad_scaled) * (sig * (1.0 + pre * (1.0 - sig)))
        msg_part = msg_part + mm_tn(message[i], grad_pre.astype(BF16))
    for p in range(rows):
        sc[p] = msg_part[p * ch:(p + 1) * ch].astype(BF16)
    one_start(2, sc, rc)

    two_start(1, sb, rb, tb, ub)
    total = three_start(0, ta, ua, fa, ch)
    g_score[...] = total[ch:ch + 1]
    two_start(2, sc, rc, tc, uc)
    three_start(1, tb, ub, fb, 3 * ch)
    three_start(2, tc, uc, fc, ch)
    three_wait(0, fa)
    for p in range(rows):
        g_out[p * ch:(p + 1) * ch] = fa[p].astype(F32)
    three_wait(1, fb)
    for p in range(rows):
        for j, out in enumerate((g_query, g_key, g_value)):
            out[p * ch:(p + 1) * ch] = fb[p, j * ch:(j + 1) * ch].astype(F32)
    three_wait(2, fc)
    for p in range(rows):
        g_msg[p * ch:(p + 1) * ch] = fc[p].astype(F32)

    for way in ways:
        @pl.when(way[3])
        def _(way=way):
            for i in range(NCH):
                halo_copy(way, i).wait_send()

    def col_send(s):
        p = lax.rem(c + s, cols)
        tok_copy(p, c).wait_send()
        ga_copy(p, c).wait_send()

    others(cols, col_send)
    finish(0, sa, ra, ta, ua, fa)
    finish(1, sb, rb, tb, ub, fb)
    finish(2, sc, rc, tc, uc, fc)


def solution(mesh):
    rows, cols = mesh.shape["row"], mesh.shape["col"]
    ch = H // rows

    def body(gate_feats, adjacency, gate_count, membership, tok_count,
             w_msg, w_query, w_key, w_value, w_out, w_score, cotangent):
        vmem = pl.BlockSpec(memory_space=pltpu.VMEM)
        smem = pl.BlockSpec(memory_space=pltpu.SMEM)
        hbm = pl.BlockSpec(memory_space=pl.ANY)
        wide = jax.ShapeDtypeStruct((H, H), F32)
        dma = pltpu.SemaphoreType.DMA
        V = pltpu.VMEM
        outs = pl.pallas_call(
            lambda *refs: kernel(rows, cols, *refs),
            out_shape=[jax.ShapeDtypeStruct((1, NT), F32), wide, wide, wide, wide, wide,
                       jax.ShapeDtypeStruct((1, H), F32)],
            in_specs=[smem, smem, hbm, hbm, hbm] + [vmem] * 7,
            out_specs=[vmem] * 7,
            scratch_shapes=[
                V((G, H), BF16), V((NCH, CG, H), BF16), V((4, NCH, CG, H), BF16),
                V((NB, 5, BLK, BLK), jnp.int32), V((NT, G), jnp.int32),
                V((NB, BLK, 5 * BLK), BF16), V((NB, BLK, 1), F32),
                V((NCH, NT, CG), BF16), V((NCH, CG, NT), BF16), V((NT, 1), F32),
                V((NCH, CG, H), BF16), V((NCH, CG, H), F32), V((NT, H), F32),
                V((NT, H), F32), V((NT, 1), F32),
                V((cols, NT, H), BF16), V((cols, NT, H), BF16), V((cols, NT, H), BF16),
                V((cols, NT, H), BF16), V((cols, NT, H), BF16),
                V((cols, HEADS, NT, NT), BF16), V((cols, HEADS, NT, NT), BF16),
                V((cols, HEADS, NT, NT), BF16),
                V((NT, H), F32), V((NT, H), F32), V((NT, H), F32), V((NT, H), F32),
                V((NT, H), F32),
                V((rows, ch + 16, H), BF16), V((rows, ch + 16, H), BF16),
                V((rows, 3 * ch, H), BF16), V((rows, 3 * ch, H), BF16),
                V((rows, ch, H), BF16), V((rows, ch, H), BF16),
                V((ch + 16, H), BF16), V((cols, ch + 16, H), BF16),
                V((3 * ch, H), BF16), V((cols, 3 * ch, H), BF16),
                V((ch, H), BF16), V((cols, ch, H), BF16),
                V((rows, ch, H), BF16), V((rows, 3 * ch, H), BF16), V((rows, ch, H), BF16),
                dma((3,)), dma((4, NCH)), dma((4, NCH)),
                dma((cols,)), dma((cols,)), dma((cols,)), dma((cols,)),
                dma((3, rows)), dma((3, rows)), dma((3, cols)), dma((3, cols)),
                dma((3, rows)), dma((3, rows)),
            ],
            compiler_params=pltpu.CompilerParams(
                collective_id=0, has_side_effects=True, vmem_limit_bytes=60 * 1024 * 1024
            ),
        )(gate_count, tok_count, gate_feats[0, 0], adjacency[0, 0], membership[0, 0],
          w_msg, w_query, w_key, w_value, w_out, w_score[None], cotangent[0])
        return (outs[0][None], *outs[1:6], outs[6][0])

    placed = (
        P("row", "col", None, None),
        P("row", "col", None, None, None, None),
        P("row", "col"),
        P("row", "col", None, None),
        P("row", "col"),
        P(), P(), P(), P(), P(), P(),
        P("row", "col", None),
    )
    return jax.shard_map(
        body,
        mesh=mesh,
        in_specs=placed,
        out_specs=(P("row", "col", None), P(), P(), P(), P(), P(), P()),
        check_vma=False,
    )
```

time: 405 us -> 112 us (0.28)
  waiting for transfers between devices: 236 us -> 0 us
  Pallas kernels: 0 us -> 98.4 us
  matrix products: 43.8 us -> 0 us
  blocking collectives: 40.9 us -> 0 us
  local copies, waits for them, and re-layouts: 48 us -> 11.4 us
  between operations: 15.7 us -> 1.94 us
  starting transfers between devices: 10.1 us -> 0 us
  other arithmetic: 8.72 us -> 0 us
    pallas_call x0 -> x1, Pallas kernels: none -> 98.4 us  [body(): pl.pallas_call(lambda *refs: kernel(rows, cols, *refs), out_shape=[jax.Sh...]
    psum x1 -> x0, waiting for transfers between devices: 92.5 us -> none  [body(): lax.psum((g_msg, g_query, g_key, g_value, g_out, g_score), ('row', 'col'))]
    all_gather x2 -> x0, waiting for transfers between devices: 70 us -> none  [the longest x1 41.9 us: body(): lax.all_gather(value_own, 'col', axis=0, tiled=True)]
    reduce_scatter x1 -> x0, waiting for transfers between devices: 45.1 us -> none  [body(): lax.psum_scatter(terms.reshape(lax.axis_size('col') * NT, 2 * H), 'col',...]
    dot_general x37 -> x0, matrix products: 43.8 us -> none  [the longest x4 9.38 us: query_grad(): jnp.einsum('hqk,khd->qhd', grad_score, split_heads(key_rows), preferred_e...]
    psum x1 -> x0, blocking collectives: 40.9 us -> none  [body(): lax.psum((g_msg, g_query, g_key, g_value, g_out, g_score), ('row', 'col'))]
    ppermute x4 -> x0, waiting for transfers between devices: 28.2 us -> none  [the longest x2 19.1 us: with_halo(): before = lax.ppermute(last, axis, up)]
    dynamic_slice x16 -> x0, local copies, waits for them, and re-layouts: 18.7 us -> none  [body(): lax.scan(add_query, zero_rows, (key_all.reshape(-1, NT, H), value_all.res...]
  transfers between devices with their start and end apart: 8 -> 0, of which waited for: 8 -> 0; matrix products, arithmetic and copies ran while one was open for 10% -> 0% of each run, Pallas kernels for 0% -> 0%
where the time goes in v1:
time: 112 us
  Pallas kernels  98.4 us (88%)
  local copies, waits for them, and re-layouts  11.4 us (10%)
  between operations  1.94 us (2%)
    pallas_call x1, Pallas kernels, body(): pl.pallas_call(lambda *refs: kernel(rows, cols, *refs), out_shape=[jax.Sh...  98.4 us
    unnamed x9, local copies, waits for them, and re-layouts  10.2 us

profile of v1, /device:TPU:0, one launch (start us, length us, event | category | flops | bytes accessed | tf_op | source)
XLA Modules:
  0.0 111.7 jit_solution(3425588211099130587)
XLA Ops:
  1.9 1.2 %broadcast_in_dim.6.refs_10_ = bf16[1,256]{1,0:T(2,128)(2,1)} reshape(bf16[256]{0:T(256)(128)(2,1)} %param.22) | data formatting | bytes 1024 | tf_op jit(solution)/shard_map/broadcast_in_dim | solution.py:419
  3.1 98.4 %shard_map.171 = (f32[1,512]{1,0:T(1,128)}, f32[256,256]{1,0:T(8,128)}, f32[256,256]{1,0:T(8,128)}, f32[256,256]{1,0:T(8,128)}, f32[256,256]{1,0:T(8,128)}, /*index=5*/f32[256,256]{1,0:T(8,128)}, f32[1,256]{1,0:T(1,128)}) custom-call(s32[1,1]{1,0:T(1,128)S(6)} %copy.26.refs_0_, s32[1,1]{1,0:T(1,128)S(6)} %copy.27.refs_1_, bf16[1024,256]{1,0:T(8,128)(2,1)} %bitcast.8, ...), custom_call_target="tpu_custom_call" | custom-call | tf_op jit(solution)/shard_map/pallas_call | solution.py:384
  101.5 0.0 copy-start
  101.5 1.3 %copy.28 = f32[1,1,512]{2,1,0:T(1,128)} copy(f32[1,1,512]{2,1,0:T(1,128)} %bitcast.10) | data formatting | bytes 4096
  102.8 1.7 %copy.29 = f32[256,256]{1,0:T(8,128)} copy(f32[256,256]{1,0:T(8,128)} %get-tuple-element.29) | data formatting | bytes 524288
  104.4 1.7 %copy.30 = f32[256,256]{1,0:T(8,128)} copy(f32[256,256]{1,0:T(8,128)} %get-tuple-element.30) | data formatting | bytes 524288
  106.1 1.7 %copy.31 = f32[256,256]{1,0:T(8,128)} copy(f32[256,256]{1,0:T(8,128)} %get-tuple-element.31) | data formatting | bytes 524288
  107.8 1.7 %copy.32 = f32[256,256]{1,0:T(8,128)} copy(f32[256,256]{1,0:T(8,128)} %get-tuple-element.32) | data formatting | bytes 524288
  109.5 1.7 %copy.33 = f32[256,256]{1,0:T(8,128)} copy(f32[256,256]{1,0:T(8,128)} %get-tuple-element.33) | data formatting | bytes 524288
  111.1 0.0 copy-done
  111.1 0.6 copy.34
Async XLA Ops:
  101.5 9.6 %copy-start = (f32[1,256]{1,0:T(1,128)S(1)}, f32[1,256]{1,0:T(1,128)}, u32[]{:S(2)}) copy-start(f32[1,256]{1,0:T(1,128)} %get-tuple-element.20) | copy-start | bytes 3076

commit v2 on v1

--- a/solution.py
+++ b/solution.py
@@ -69,7 +69,7 @@
     rows, cols,
     gate_count, tok_count, feats_hbm, adj_hbm, mem_hbm,
     w_msg, w_query, w_key, w_value, w_out, w_score, cot,
-    value_out, g_msg, g_query, g_key, g_value, g_out, g_score,
+    value_out, g_score, out_a, out_b, out_c,
     feats, live, halo, adj_i, mem_i, adj, inv_deg, mem, mem_t, inv_cnt,
     message, preact, pooled, normed, rscale,
     tok, q_all, k_all, v_all, ga_all, d_own, p_t, d_t, att, gq, gk, gv, gmix,
@@ -175,21 +175,63 @@
     rscale[...] = rs_val
     tok[c] = (tlive * norm_val).astype(BF16)
 
-    def tok_copy(peer, slot):
-        return remote(tok.at[slot], tok.at[slot], tok_s.at[peer], tok_r.at[slot], "col", peer)
-
-    others(cols, lambda s: tok_copy(lax.rem(c + s, cols), c).start())
     own_tok = tok[c]
+    half = NT // 2
+
+    def chain_copy(buf, send, recv, src, k, step):
+        part = buf.at[src, pl.ds(k * half, half)]
+        return remote(part, part, send.at[src, k], recv.at[src, k], "col", c + step)
+
+    def chain(buf, send, recv):
+        def own(action):
+            @pl.when(c < cols - 1)
+            def _():
+                for k in range(2):
+                    action(chain_copy(buf, send.at[0], recv, c, k, 1))
+
+            @pl.when(c > 0)
+            def _():
+                for k in range(2):
+                    action(chain_copy(buf, send.at[1], recv, c, k, -1))
+
+        def on(src, lane, step, more, wait):
+            for k in range(2):
+                if wait:
+                    chain_copy(buf, send.at[lane], recv, src, k, -step).wait_recv()
+
+                @pl.when(more)
+                def _(k=k):
+                    copy = chain_copy(buf, send.at[lane], recv, src, k, step)
+                    copy.start() if wait else copy.wait_send()
+
+        def hop(d, wait=True):
+            @pl.when(c - d >= 0)
+            def _():
+                on(c - d, 0, 1, c < cols - 1, wait)
+
+            @pl.when(c + d < cols)
+            def _():
+                on(c + d, 1, -1, c > 0, wait)
+
+        return own, hop
+
+    def at_distance(d, func):
+        @pl.when(c - d >= 0)
+        def _():
+            func(c - d)
+
+        @pl.when(c + d < cols)
+        def _():
+            func(c + d)
+
+    tok_own, tok_hop = chain(tok, tok_s, tok_r)
+    ga_own, ga_hop = chain(ga_all, ga_s, ga_r)
+    tok_own(lambda copy: copy.start())
+
     q_all[c] = mm(own_tok, w_query[...]).astype(BF16)
     att[...] = jnp.zeros((NT, H), F32)
 
-    def attend_step(s, carry):
-        src = lax.rem(c + s, cols)
-
-        @pl.when(s > 0)
-        def _():
-            tok_copy(src, src).wait_recv()
-
+    def attend(src):
         k_all[src] = mm(tok[src], w_key[...]).astype(BF16)
         v_all[src] = mm(tok[src], w_value[...]).astype(BF16)
         for h in range(HEADS):
@@ -197,9 +239,32 @@
             prob, slope = prob_parts(mm_nt(q_all[c, :, lanes], k_all[src, :, lanes]))
             d_own[src, h] = slope.astype(BF16)
             att[:, lanes] += mm(prob.astype(BF16), v_all[src, :, lanes])
-        return carry
-
-    lax.fori_loop(0, cols, attend_step, 0)
+
+    def key_probs(src):
+        for h in range(HEADS):
+            lanes = slice(h * HD, (h + 1) * HD)
+            prob, slope = prob_parts(mm_nt(k_all[c, :, lanes], q_all[src, :, lanes]))
+            p_t[src, h] = prob.astype(BF16)
+            d_t[src, h] = slope.astype(BF16)
+
+    def key_probs_of(src):
+        q_all[src] = mm(tok[src], w_query[...]).astype(BF16)
+        key_probs(src)
+
+    attend(c)
+    key_probs(c)
+
+    def attend_step(d, carry):
+        tok_hop(d)
+        at_distance(d, attend)
+
+        @pl.when(d < cols - 1)
+        def _():
+            at_distance(d, key_probs_of)
+
+        return carry
+
+    lax.fori_loop(1, cols, attend_step, 0)
 
     attended = att[...].astype(BF16)
     pnormed, pscale = rms_forward(mm(attended, w_out[...]))
@@ -214,10 +279,7 @@
     grad_proj = rms_backward(grad_mixed, pnormed, pscale).astype(BF16)
     ga_all[c] = mm_nt(grad_proj, w_out[...]).astype(BF16)
 
-    def ga_copy(peer, slot):
-        return remote(ga_all.at[slot], ga_all.at[slot], ga_s.at[peer], ga_r.at[slot], "col", peer)
-
-    others(cols, lambda s: ga_copy(lax.rem(c + s, cols), c).start())
+    ga_own(lambda copy: copy.start())
 
     def one_copy(g, send, recv, peer, slot):
         return remote(send.at[peer], recv.at[slot], one_s.at[g, peer], one_r.at[g, slot], "row", peer)
@@ -270,60 +332,62 @@
     out_part = mm_tn(attended, grad_proj)
     for p in range(rows):
         sa[p, 0:ch] = out_part[p * ch:(p + 1) * ch].astype(BF16)
-        sa[p, ch:ch + 16] = score_part.astype(BF16)
-    one_start(0, sa, ra)
+        sa[p, 2 * ch:2 * ch + 16] = score_part.astype(BF16)
 
     gq[...] = jnp.zeros((NT, H), F32)
     gk[...] = jnp.zeros((NT, H), F32)
     gv[...] = jnp.zeros((NT, H), F32)
 
-    def query_step(s, carry):
-        src = lax.rem(c + s, cols)
-        q_all[src] = mm(tok[src], w_query[...]).astype(BF16)
+    def query_step(src, carry):
         for h in range(HEADS):
             lanes = slice(h * HD, (h + 1) * HD)
             grad_prob = mm_nt(ga_all[c, :, lanes], v_all[src, :, lanes])
             grad_score = (grad_prob * d_own[src, h].astype(F32)).astype(BF16)
             gq[:, lanes] += mm(grad_score, k_all[src, :, lanes])
-            prob, slope = prob_parts(mm_nt(k_all[c, :, lanes], q_all[src, :, lanes]))
-            p_t[src, h] = prob.astype(BF16)
-            d_t[src, h] = slope.astype(BF16)
         return carry
 
     lax.fori_loop(0, cols, query_step, 0)
-    two_start(0, sa, ra, ta, ua)
-
-    def key_step(s, carry):
-        src = lax.rem(c + s, cols)
-
-        @pl.when(s > 0)
-        def _():
-            ga_copy(src, src).wait_recv()
-
+    grad_query = gq[...].astype(BF16)
+    part = mm_tn(own_tok, grad_query).astype(BF16)
+    for p in range(rows):
+        sa[p, ch:2 * ch] = part[p * ch:(p + 1) * ch]
+    one_start(0, sa, ra)
+
+    def key_grads(src):
         for h in range(HEADS):
             lanes = slice(h * HD, (h + 1) * HD)
             grad_prob = mm_nt(v_all[c, :, lanes], ga_all[src, :, lanes])
             grad_score = (grad_prob * d_t[src, h].astype(F32)).astype(BF16)
             gk[:, lanes] += mm(grad_score, q_all[src, :, lanes])
             gv[:, lanes] += mm(p_t[src, h], ga_all[src, :, lanes])
-        return carry
-
-    lax.fori_loop(0, cols, key_step, 0)
-
-    grad_query = gq[...].astype(BF16)
+
+    def key_step(d, carry):
+        ga_hop(d)
+        at_distance(d, key_grads)
+        return carry
+
+    ga_hop(1)
+    at_distance(cols - 1, key_probs_of)
+    key_grads(c)
+    at_distance(1, key_grads)
+    two_start(0, sa, ra, ta, ua)
+    gmix[...] += mm_nt(grad_query, w_query[...])
+    lax.fori_loop(2, cols, key_step, 0)
+
     grad_key = gk[...].astype(BF16)
     grad_val = gv[...].astype(BF16)
-    for j, grad in enumerate((grad_query, grad_key, grad_val)):
+    for j, grad in enumerate((grad_key, grad_val)):
         part = mm_tn(own_tok, grad).astype(BF16)
         for p in range(rows):
             sb[p, j * ch:(j + 1) * ch] = part[p * ch:(p + 1) * ch]
     one_start(1, sb, rb)
 
-    grad_tokens = gmix[...] + mm_nt(grad_query, w_query[...])
-    grad_tokens = grad_tokens + mm_nt(grad_key, w_key[...])
+    grad_tokens = gmix[...] + mm_nt(grad_key, w_key[...])
     grad_tokens = grad_tokens + mm_nt(grad_val, w_value[...])
     grad_pooled = rms_backward(tlive * grad_tokens, normed[...], rscale[...])
     grad_scaled = (grad_pooled * inv_cnt[...]).astype(BF16)
+    total = three_start(0, ta, ua, fa, 2 * ch)
+    g_score[...] = total[2 * ch:2 * ch + 1]
     msg_part = jnp.zeros((H, H), F32)
     for i in range(NCH):
         alive = (lax.broadcasted_iota(jnp.int32, (CG, 1), 0) + i * CG < gates).astype(F32)
@@ -334,23 +398,16 @@
     for p in range(rows):
         sc[p] = msg_part[p * ch:(p + 1) * ch].astype(BF16)
     one_start(2, sc, rc)
-
     two_start(1, sb, rb, tb, ub)
-    total = three_start(0, ta, ua, fa, ch)
-    g_score[...] = total[ch:ch + 1]
     two_start(2, sc, rc, tc, uc)
-    three_start(1, tb, ub, fb, 3 * ch)
+    three_start(1, tb, ub, fb, 2 * ch)
     three_start(2, tc, uc, fc, ch)
     three_wait(0, fa)
-    for p in range(rows):
-        g_out[p * ch:(p + 1) * ch] = fa[p].astype(F32)
+    out_a[...] = fa[...]
     three_wait(1, fb)
-    for p in range(rows):
-        for j, out in enumerate((g_query, g_key, g_value)):
-            out[p * ch:(p + 1) * ch] = fb[p, j * ch:(j + 1) * ch].astype(F32)
+    out_b[...] = fb[...]
     three_wait(2, fc)
-    for p in range(rows):
-        g_msg[p * ch:(p + 1) * ch] = fc[p].astype(F32)
+    out_c[...] = fc[...]
 
     for way in ways:
         @pl.when(way[3])
@@ -358,15 +415,32 @@
             for i in range(NCH):
                 halo_copy(way, i).wait_send()
 
-    def col_send(s):
-        p = lax.rem(c + s, cols)
-        tok_copy(p, c).wait_send()
-        ga_copy(p, c).wait_send()
-
-    others(cols, col_send)
+    tok_own(lambda copy: copy.wait_send())
+    ga_own(lambda copy: copy.wait_send())
+
+    def sent(d, carry):
+        tok_hop(d, False)
+        ga_hop(d, False)
+        return carry
+
+    lax.fori_loop(1, cols, sent, 0)
     finish(0, sa, ra, ta, ua, fa)
     finish(1, sb, rb, tb, ub, fb)
     finish(2, sc, rc, tc, uc, fc)
+
+
+def unpack(rows, value_in, score_in, in_a, in_b, in_c,
+           value_out, g_msg, g_query, g_key, g_value, g_out, g_score):
+    ch = H // rows
+    value_out[0] = value_in[...]
+    g_score[...] = score_in[...]
+    for p in range(rows):
+        cut = slice(p * ch, (p + 1) * ch)
+        g_out[cut] = in_a[p, 0:ch].astype(F32)
+        g_query[cut] = in_a[p, ch:2 * ch].astype(F32)
+        g_key[cut] = in_b[p, 0:ch].astype(F32)
+        g_value[cut] = in_b[p, ch:2 * ch].astype(F32)
+        g_msg[cut] = in_c[p].astype(F32)
 
 
 def solution(mesh):
@@ -383,10 +457,10 @@
         V = pltpu.VMEM
         outs = pl.pallas_call(
             lambda *refs: kernel(rows, cols, *refs),
-            out_shape=[jax.ShapeDtypeStruct((1, NT), F32), wide, wide, wide, wide, wide,
-                       jax.ShapeDtypeStruct((1, H), F32)],
+            out_shape=[jax.ShapeDtypeStruct((1, NT), F32), jax.ShapeDtypeStruct((1, H), F32)]
+            + [jax.ShapeDtypeStruct((rows, n * ch, H), BF16) for n in (2, 2, 1)],
             in_specs=[smem, smem, hbm, hbm, hbm] + [vmem] * 7,
-            out_specs=[vmem] * 7,
+            out_specs=[vmem] * 5,
             scratch_shapes=[
                 V((G, H), BF16), V((NCH, CG, H), BF16), V((4, NCH, CG, H), BF16),
                 V((NB, 5, BLK, BLK), jnp.int32), V((NT, G), jnp.int32),
@@ -400,15 +474,15 @@
                 V((cols, HEADS, NT, NT), BF16),
                 V((NT, H), F32), V((NT, H), F32), V((NT, H), F32), V((NT, H), F32),
                 V((NT, H), F32),
-                V((rows, ch + 16, H), BF16), V((rows, ch + 16, H), BF16),
-                V((rows, 3 * ch, H), BF16), V((rows, 3 * ch, H), BF16),
+                V((rows, 2 * ch + 16, H), BF16), V((rows, 2 * ch + 16, H), BF16),
+                V((rows, 2 * ch, H), BF16), V((rows, 2 * ch, H), BF16),
                 V((rows, ch, H), BF16), V((rows, ch, H), BF16),
-                V((ch + 16, H), BF16), V((cols, ch + 16, H), BF16),
-                V((3 * ch, H), BF16), V((cols, 3 * ch, H), BF16),
+                V((2 * ch + 16, H), BF16), V((cols, 2 * ch + 16, H), BF16),
+                V((2 * ch, H), BF16), V((cols, 2 * ch, H), BF16),
                 V((ch, H), BF16), V((cols, ch, H), BF16),
-                V((rows, ch, H), BF16), V((rows, 3 * ch, H), BF16), V((rows, ch, H), BF16),
+                V((rows, 2 * ch, H), BF16), V((rows, 2 * ch, H), BF16), V((rows, ch, H), BF16),
                 dma((3,)), dma((4, NCH)), dma((4, NCH)),
-                dma((cols,)), dma((cols,)), dma((cols,)), dma((cols,)),
+                dma((2, cols, 2)), dma((cols, 2)), dma((2, cols, 2)), dma((cols, 2)),
                 dma((3, rows)), dma((3, rows)), dma((3, cols)), dma((3, cols)),
                 dma((3, rows)), dma((3, rows)),
             ],
@@ -417,7 +491,14 @@
             ),
         )(gate_count, tok_count, gate_feats[0, 0], adjacency[0, 0], membership[0, 0],
           w_msg, w_query, w_key, w_value, w_out, w_score[None], cotangent[0])
-        return (outs[0][None], *outs[1:6], outs[6][0])
+        done = pl.pallas_call(
+            lambda *refs: unpack(rows, *refs),
+            out_shape=[jax.ShapeDtypeStruct((1, 1, NT), F32), wide, wide, wide, wide, wide,
+                       jax.ShapeDtypeStruct((1, H), F32)],
+            in_specs=[vmem] * 5,
+            out_specs=[vmem] * 7,
+        )(*outs)
+        return (*done[:6], done[6][0])
 
     placed = (
         P("row", "col", None, None),

time: 112 us -> 88.6 us (0.79)
  Pallas kernels: 98.4 us -> 84.6 us
  local copies, waits for them, and re-layouts: 11.4 us -> 1.22 us
    pallas_call x1, Pallas kernels: 98.4 us -> 82.4 us  [body(): pl.pallas_call(lambda *refs: kernel(rows, cols, *refs), out_shape=[jax.Sh...]
    unnamed x9 -> x0, local copies, waits for them, and re-layouts: 10.2 us -> none
    pallas_call x0 -> x1, Pallas kernels: none -> 2.18 us  [body(): pl.pallas_call(lambda *refs: unpack(rows, *refs), out_shape=[jax.ShapeDty...]
where the time goes in v2:
time: 88.6 us; the launch traced here: 87.8 us
  Pallas kernels  84.6 us (95%)
  between operations  1.93 us (2%)
  local copies, waits for them, and re-layouts  1.22 us (1%)
    pallas_call x1, Pallas kernels, body(): pl.pallas_call(lambda *refs: kernel(rows, cols, *refs), out_shape=[jax.Sh...  82.4 us
    pallas_call x1, Pallas kernels, body(): pl.pallas_call(lambda *refs: unpack(rows, *refs), out_shape=[jax.ShapeDty...  2.18 us

profile of v2, /device:TPU:0, one launch (start us, length us, event | category | flops | bytes accessed | tf_op | source)
XLA Modules:
  0.0 87.8 jit_solution(7088051177291853572)
XLA Ops:
  1.9 1.2 %broadcast_in_dim.3.refs_10_ = bf16[1,256]{1,0:T(2,128)(2,1)} reshape(bf16[256]{0:T(256)(128)(2,1)} %param.22) | data formatting | bytes 1024 | tf_op jit(solution)/shard_map/broadcast_in_dim | solution.py:493
  3.1 82.4 %shard_map.171 = (f32[1,512]{1,0:T(1,128)}, f32[1,256]{1,0:T(1,128)}, bf16[8,64,256]{2,1,0:T(8,128)(2,1)}, bf16[8,64,256]{2,1,0:T(8,128)(2,1)}, bf16[8,32,256]{2,1,0:T(8,128)(2,1)}) custom-call(s32[1,1]{1,0:T(1,128)S(6)} %copy.19.refs_0_, s32[1,1]{1,0:T(1,128)S(6)} %copy.20.refs_1_, bf16[1024,256]{1,0:T(8,128)(2,1)} %bitcast.7, s32[8,5,128,128]{3,2,1,0:T(8,128)} %bitcast.5, ...), custom_call_target="tpu_custom_call" | custom-call | tf_op jit(solution)/shard_map/pallas_call | solution.py:458
  85.6 2.2 %shard_map.172 = (f32[1,1,512]{2,1,0:T(1,128)}, f32[256,256]{1,0:T(8,128)}, f32[256,256]{1,0:T(8,128)}, f32[256,256]{1,0:T(8,128)}, f32[256,256]{1,0:T(8,128)}, /*index=5*/f32[256,256]{1,0:T(8,128)}, f32[1,256]{1,0:T(1,128)}) custom-call(f32[1,512]{1,0:T(1,128)} %get-tuple-element.19.refs_0_, f32[1,256]{1,0:T(1,128)} %get-tuple-element.20.refs_1_, ...), custom_call_target="tpu_custom_call" | custom-call | tf_op jit(solution)/shard_map/pallas_call | solution.py:494
